TPU v7x, 128 devices: a whole 4x4x4 slice. The times are simulated.
128 devices in a mesh: row: 8 (over y, core), col: 16 (over x, z).
Axes of the slice: x: 4, y: 4, z: 4, core: 2. Of those that a mesh axis runs over, the one named last changes fastest.
Arguments:
- x_blocks: bfloat16 [8, 16, 16, 128, 1024], P('row', 'col'), may hold values from -6 to 6
- factors: bfloat16 [8, 16, 16, 11, 2, 128, 128], P('row', 'col'), may hold values from -0.375 to 0.375
- pattern: int32 [8, 16, 16, 11], P('row', 'col'), may hold values 0 or 1
Outputs:
- result: bfloat16 [8, 16, 16, 128, 1024], P('row', 'col')
All inputs are finite; a program needn't handle non-finite values. No bound on the sum of `pattern` on one device may be relied on, other than what follows from the above.
Results may differ from a plain program's by a relative error of at most 0.02.
Values may be sent and summed in bfloat16 or wider, within the bound.
A program may use at most 128 MiB of HBM per device.

v0:
```python
import jax
import jax.numpy as jnp
from jax import lax
from jax.sharding import PartitionSpec as P


def swapped(value, axis, bit):
    mask = 2**bit
    pairs = [(source, source ^ mask) for source in range(lax.axis_size(axis))]
    return lax.ppermute(value, axis, pairs)


def flipped(array, bit):
    count = array.shape[0]
    return array.reshape((count >> bit + 1, 2, 1 << bit) + array.shape[1:])[:, ::-1].reshape(
        array.shape
    )


def combine(current, partner, level_w, alive):
    own = jnp.einsum("nij,njr->nir", level_w[:, 0], current, preferred_element_type=jnp.float32)
    cross = jnp.einsum("nij,njr->nir", level_w[:, 1], partner, preferred_element_type=jnp.float32)
    return (own + alive.astype(jnp.float32)[:, None, None] * cross).astype(jnp.bfloat16)


def on_device(x_blocks, factors, pattern):
    blocks = x_blocks.shape[2]
    order = x_blocks.shape[3]
    width = x_blocks.shape[4]
    levels = factors.shape[3]
    current = x_blocks.reshape(blocks, order, width)
    weights = factors.reshape(blocks, levels, 2, order, order)
    active = pattern.reshape(blocks, levels)
    local_levels = blocks.bit_length() - 1
    col_groups = lax.axis_size("col")
    row_groups = lax.axis_size("row")
    col_count = col_groups.bit_length() - 1
    row_count = row_groups.bit_length() - 1
    for level in range(local_levels):
        current = combine(current, flipped(current, level), weights[:, level], active[:, level])
    first_row = local_levels + col_count
    for bit in range(col_count):
        partner = swapped(current, "col", bit)
        current = combine(
            current, partner, weights[:, local_levels + bit], active[:, local_levels + bit]
        )
    for bit in range(row_count):
        partner = swapped(current, "row", bit)
        current = combine(current, partner, weights[:, first_row + bit], active[:, first_row + bit])
    return current.reshape(1, 1, blocks, order, width)


def solution(mesh):
    return jax.shard_map(
        on_device,
        mesh=mesh,
        in_specs=(
            P("row", "col", None, None, None),
            P("row", "col", None, None, None, None, None),
            P("row", "col", None, None),
        ),
        out_specs=P("row", "col", None, None, None),
        check_vma=False,
    )
```

profile of v0, /device:TPU:1, one launch (start us, length us, event | category | flops | bytes accessed | tf_op | source)
XLA Modules:
  0.0 635.0 jit_solution(15337389907191785998)
XLA Ops:
  0.0 0.7 copy.13
  0.7 4.8 rev.12
  5.5 6.2 copy.12
  11.7 0.0 copy-start
  11.7 3.7 slice_bitcast_fusion
  15.4 1.0 copy-done
  16.5 1.2 fusion.1
  17.7 0.9 copy-done.1
  18.7 3.3 add_convert_fusion.10
  21.9 4.7 rev.13
  26.7 0.0 copy-start.2
  26.7 0.0 copy-start.11
  26.7 3.8 fusion.12
  30.5 0.0 copy-done.2
  30.5 0.1 copy-done.11
  30.6 4.4 add_convert_fusion.9
  34.9 4.5 rev.14
  39.5 0.0 copy-start.3
  39.5 3.7 fusion.11
  43.2 0.0 copy-done.3
  43.2 0.2 copy-done.10
  43.4 3.3 add_convert_fusion.8
  46.6 4.5 rev.15
  51.2 0.0 copy-start.4
  51.2 0.0 copy-start.9
  51.2 3.7 fusion.10
  54.9 0.0 copy-done.4
  54.9 0.2 copy-done.9
  55.1 0.0 copy-start.8
  55.1 1.4 add_convert_fusion.7
  56.5 2.5 collective-permute-start
  59.1 0.0 copy-done.8
  59.1 1.2 fusion.9
  60.3 89.0 %collective-permute-done = bf16[16,128,1024]{1,2,0:T(8,128)(2,1)S(1)} collective-permute-done((bf16[16,128,1024]{1,2,0:T(8,128)(2,1)S(1)}, bf16[16,128,1024]{1,2,0:T(8,128)(2,1)S(1)}, u32[]{:S(2)}, u32[]{:S(2)}) %collective-permute-start) | collective-permute-done | bytes 4194336 | tf_op jit(solution)/shard_map/ppermute | solution.py:10
  149.4 0.0 copy-start.7
  149.4 1.3 add_convert_fusion.6
  150.6 3.2 collective-permute-start.1
  153.8 0.0 copy-done.7
  153.8 1.3 fusion.8
  155.1 88.1 %collective-permute-done.1 = bf16[16,128,1024]{1,2,0:T(8,128)(2,1)S(1)} collective-permute-done((bf16[16,128,1024]{1,2,0:T(8,128)(2,1)S(1)}, bf16[16,128,1024]{1,2,0:T(8,128)(2,1)S(1)}, u32[]{:S(2)}, u32[]{:S(2)}) %collective-permute-start.1) | collective-permute-done | bytes 4194336 | tf_op jit(solution)/shard_map/ppermute | solution.py:10
  243.2 1.3 add_convert_fusion.5
  244.4 1.3 collective-permute-start.2
  245.7 0.0 copy-done.6
  245.7 1.2 fusion.7
  247.0 87.4 %collective-permute-done.2 = bf16[16,128,1024]{1,2,0:T(8,128)(2,1)S(1)} collective-permute-done((bf16[16,128,1024]{1,2,0:T(8,128)(2,1)S(1)}, bf16[16,128,1024]{1,2,0:T(8,128)(2,1)S(1)}, u32[]{:S(2)}, u32[]{:S(2)}) %collective-permute-start.2) | collective-permute-done | bytes 4194336 | tf_op jit(solution)/shard_map/ppermute | solution.py:10
  334.4 1.3 add_convert_fusion.4
  335.6 2.8 collective-permute-start.3
  338.5 0.0 copy-done.5
  338.5 1.3 fusion.6
  339.7 86.4 %collective-permute-done.3 = bf16[16,128,1024]{1,2,0:T(8,128)(2,1)S(1)} collective-permute-done((bf16[16,128,1024]{1,2,0:T(8,128)(2,1)S(1)}, bf16[16,128,1024]{1,2,0:T(8,128)(2,1)S(1)}, u32[]{:S(2)}, u32[]{:S(2)}) %collective-permute-start.3) | collective-permute-done | bytes 4194336 | tf_op jit(solution)/shard_map/ppermute | solution.py:10
  426.2 1.3 add_convert_fusion.3
  427.4 4.3 collective-permute-start.4
  431.8 1.3 fusion.5
  433.0 5.5 collective-permute-done.4
  438.6 1.3 add_convert_fusion.2
  439.8 1.4 collective-permute-start.5
  441.2 1.3 fusion.4
  442.5 89.2 %collective-permute-done.5 = bf16[16,128,1024]{1,2,0:T(8,128)(2,1)S(1)} collective-permute-done((bf16[16,128,1024]{1,2,0:T(8,128)(2,1)S(1)}, bf16[16,128,1024]{1,2,0:T(8,128)(2,1)S(1)}, u32[]{:S(2)}, u32[]{:S(2)}) %collective-permute-start.5) | collective-permute-done | bytes 4194336 | tf_op jit(solution)/shard_map/ppermute | solution.py:10
  531.7 1.3 add_convert_fusion.1
  533.0 3.0 collective-permute-start.6
  536.0 1.3 fusion.3
  537.2 88.2 %collective-permute-done.6 = bf16[16,128,1024]{1,2,0:T(8,128)(2,1)S(1)} collective-permute-done((bf16[16,128,1024]{1,2,0:T(8,128)(2,1)S(1)}, bf16[16,128,1024]{1,2,0:T(8,128)(2,1)S(1)}, u32[]{:S(2)}, u32[]{:S(2)}) %collective-permute-start.6) | collective-permute-done | bytes 4194336 | tf_op jit(solution)/shard_map/ppermute | solution.py:10
  625.4 3.2 fusion
  628.6 6.4 %copy.7 = bf16[1,1,16,128,1024]{4,3,2,1,0:T(8,128)(2,1)} copy(bf16[1,1,16,128,1024]{3,4,2,1,0:T(8,128)(2,1)} %fusion) | data formatting | bytes 8388608 | tf_op jit(solution)/shard_map/reshape | solution.py:50
  (5 shorter events, 0.0 us)
Async XLA Ops:
  11.7 4.7 copy-start
  16.5 2.2 copy-start.1
  26.7 3.8 copy-start.2
  26.7 3.9 copy-start.11
  39.5 3.7 copy-start.3
  39.5 3.9 copy-start.10
  51.2 3.7 copy-start.4
  51.2 3.9 copy-start.9
  55.1 4.0 copy-start.8
  56.5 92.8 %collective-permute-start = (bf16[16,128,1024]{1,2,0:T(8,128)(2,1)S(1)}, bf16[16,128,1024]{1,2,0:T(8,128)(2,1)S(1)}, u32[]{:S(2)}, u32[]{:S(2)}) collective-permute-start(bf16[16,128,1024]{1,2,0:T(8,128)(2,1)S(1)} %bitcast.169), channel_id=1, source_target_pairs={{0,1},{1,0},{2,3},{3,2},{4,5},{5,4},{6,7},{7,6},{8,9},{9,8},{10,11... | collective-permute-start | bytes 12582920 | tf_op jit(solution)/shard_map/ppermute | solution.py:10
  149.4 4.5 copy-start.7
  150.6 92.5 %collective-permute-start.1 = (bf16[16,128,1024]{1,2,0:T(8,128)(2,1)S(1)}, bf16[16,128,1024]{1,2,0:T(8,128)(2,1)S(1)}, u32[]{:S(2)}, u32[]{:S(2)}) collective-permute-start(bf16[16,128,1024]{1,2,0:T(8,128)(2,1)S(1)} %bitcast.170), channel_id=1, source_target_pairs={{0,2},{1,3},{2,0},{3,1},{4,6},{5,7},{6,4},{7,5},{8,10},{9,11},{10,... | collective-permute-start | bytes 12582920 | tf_op jit(solution)/shard_map/ppermute | solution.py:10
  243.2 2.5 copy-start.6
  244.4 90.0 %collective-permute-start.2 = (bf16[16,128,1024]{1,2,0:T(8,128)(2,1)S(1)}, bf16[16,128,1024]{1,2,0:T(8,128)(2,1)S(1)}, u32[]{:S(2)}, u32[]{:S(2)}) collective-permute-start(bf16[16,128,1024]{1,2,0:T(8,128)(2,1)S(1)} %bitcast.171), channel_id=1, source_target_pairs={{0,4},{1,5},{2,6},{3,7},{4,0},{5,1},{6,2},{7,3},{8,12},{9,13},{10,... | collective-permute-start | bytes 12582920 | tf_op jit(solution)/shard_map/ppermute | solution.py:10
  334.4 4.1 copy-start.5
  335.6 90.5 %collective-permute-start.3 = (bf16[16,128,1024]{1,2,0:T(8,128)(2,1)S(1)}, bf16[16,128,1024]{1,2,0:T(8,128)(2,1)S(1)}, u32[]{:S(2)}, u32[]{:S(2)}) collective-permute-start(bf16[16,128,1024]{1,2,0:T(8,128)(2,1)S(1)} %bitcast.172), channel_id=1, source_target_pairs={{0,8},{1,9},{2,10},{3,11},{4,12},{5,13},{6,14},{7,15},{8,0},{9,1},... | collective-permute-start | bytes 12582920 | tf_op jit(solution)/shard_map/ppermute | solution.py:10
  427.4 11.1 %collective-permute-start.4 = (bf16[16,128,1024]{1,2,0:T(8,128)(2,1)S(1)}, bf16[16,128,1024]{1,2,0:T(8,128)(2,1)S(1)}, u32[]{:S(2)}, u32[]{:S(2)}) collective-permute-start(bf16[16,128,1024]{1,2,0:T(8,128)(2,1)S(1)} %bitcast.173), channel_id=1, source_target_pairs={{0,16},{16,0},{32,48},{48,32},{64,80},{80,64},{96,112},{112,96},{1... | collective-permute-start | bytes 12582920 | tf_op jit(solution)/shard_map/ppermute | solution.py:10
  439.8 91.9 %collective-permute-start.5 = (bf16[16,128,1024]{1,2,0:T(8,128)(2,1)S(1)}, bf16[16,128,1024]{1,2,0:T(8,128)(2,1)S(1)}, u32[]{:S(2)}, u32[]{:S(2)}) collective-permute-start(bf16[16,128,1024]{1,2,0:T(8,128)(2,1)S(1)} %bitcast.174), channel_id=1, source_target_pairs={{0,32},{16,48},{32,0},{48,16},{64,96},{80,112},{96,64},{112,80},{1... | collective-permute-start | bytes 12582920 | tf_op jit(solution)/shard_map/ppermute | solution.py:10
  533.0 92.4 %collective-permute-start.6 = (bf16[16,128,1024]{1,2,0:T(8,128)(2,1)S(1)}, bf16[16,128,1024]{1,2,0:T(8,128)(2,1)S(1)}, u32[]{:S(2)}, u32[]{:S(2)}) collective-permute-start(bf16[16,128,1024]{1,2,0:T(8,128)(2,1)S(1)} %bitcast.168), channel_id=1, source_target_pairs={{0,64},{16,80},{32,96},{48,112},{64,0},{80,16},{96,32},{112,48},{1... | collective-permute-start | bytes 12582920 | tf_op jit(solution)/shard_map/ppermute | solution.py:10
where the time goes:
time: 636 us; the launch traced here: 635 us
  waiting for transfers between devices  534 us (84%)
  matrix products  44.3 us (7%)
  local copies, waits for them, and re-layouts  38.1 us (6%)
  starting transfers between devices  18.6 us (3%)
    ppermute x7, waiting for transfers between devices, swapped(): return lax.ppermute(value, axis, pairs)  534 us
    dot_general x11, matrix products, combine(): jnp.einsum('nij,njr->nir', level_w[:, 1], partner, preferred_element_type...  23.1 us
    dot_general x11, matrix products, combine(): jnp.einsum('nij,njr->nir', level_w[:, 0], current, preferred_element_type...  21.2 us
    rev x4, local copies, waits for them, and re-layouts, flipped(): array.reshape((count >> bit + 1, 2, 1 << bit) + array.shape[1:])[:, ::-1]  18.6 us
    ppermute x7, starting transfers between devices, swapped(): return lax.ppermute(value, axis, pairs)  18.6 us
  transfers between devices with their start and end apart: 7, of which 7 were waited for; matrix products, arithmetic and copies ran while one was open for 1% of the time, Pallas kernels for 0%

commit v1 on v0

v1 whole, which is shorter than its diff:
```python
import functools

import jax
import jax.numpy as jnp
from jax import lax
from jax.experimental import pallas as pl
from jax.experimental.pallas import tpu as pltpu
from jax.sharding import PartitionSpec as P

MESH = pl.DeviceIdType.MESH
B = 128
W = 128
WL = 256
GROUPS = 4
DEPTH = 4
OFF = (0, 2, 4, 6, 8, 10, 12, 14)


def dot(lhs, rhs):
    return jnp.dot(lhs, rhs, preferred_element_type=jnp.float32).astype(jnp.bfloat16)


def side(p):
    return lax.rem(lax.rem(p, 2) + lax.div(p, 2), 2)


def flip(p):
    return p + 1 - 2 * lax.rem(p, 2)


def kernel(
    pat, x_hbm, f_hbm, out, H, FAC, FRZ, FRX, FRC, FRY,
    R1, R2, R3, R4, R5, R6, R7, S1, S2, S3, S4, S5, S6, S7,
    xs, fs, frs, fss,
    r1, r2, r3, r4, r5, r6, r7, r8, s1, s2, s3, s4, s5, s6, s7, s8, os,
):
    width = H.shape[4]
    chunks = width // W
    units = GROUPS * chunks
    row = lax.axis_index("row")
    col = lax.axis_index("col")
    y, c = lax.div(row, 2), lax.rem(row, 2)
    xx, z = lax.div(col, 4), lax.rem(col, 4)
    sz, sx, sy = side(z), side(xx), side(y)

    def dev(z_, x_, y_, c_):
        return (y_ * 2 + c_, x_ * 4 + z_)

    fz, fx, fy, fc = flip(z), flip(xx), flip(y), 1 - c
    Z1, Z3 = dev(fz, xx, y, c), dev(3 - z, xx, y, c)
    X1, X3 = dev(z, fx, y, c), dev(z, 3 - xx, y, c)
    Y1, Y3 = dev(z, xx, fy, c), dev(z, xx, 3 - y, c)
    C1 = dev(z, xx, y, fc)
    ZX, XC, YC = dev(fz, fx, y, c), dev(z, fx, y, fc), dev(z, xx, fy, fc)

    def send(src, dst, ssem, rsem, to):
        return pltpu.make_async_remote_copy(
            src_ref=src, dst_ref=dst, send_sem=ssem, recv_sem=rsem, device_id=to, device_id_type=MESH
        )

    def load_f(k):
        return pltpu.make_async_copy(f_hbm.at[:, k], FAC.at[:, k], fs.at[k])

    def load_x(i):
        cols = pl.ds(i * WL, WL)
        return pltpu.make_async_copy(x_hbm.at[:, :, :, :, cols], H.at[:, :, :, :, cols], xs.at[i])

    for k in (4, 5, 0):
        load_f(k).start()
    load_x(0).start()
    for k in (1, 2, 3):
        load_f(k).start()
    for i in range(1, width // WL):
        load_x(i).start()
    for k in (6, 7, 8, 9, 10):
        load_f(k).start()

    barrier = pltpu.get_barrier_semaphore()
    partners = (Z1, Z3, ZX, X1, X3, XC, C1, YC, Y1, Y3)
    for to in partners:
        pl.semaphore_signal(barrier, inc=1, device_id=to, device_id_type=MESH)

    def scale(levels):
        def body(l, carry):
            for k in levels:
                m = pat[0, 0, l, k].astype(jnp.float32)
                FAC[l, k, 1] = (FAC[l, k, 1].astype(jnp.float32) * m).astype(jnp.bfloat16)
            return carry

        lax.fori_loop(0, 4 * GROUPS, body, 0)

    def f_z(g, j):
        return send(
            FAC.at[4 * g + 2 * j + 1 - sz, 4:6], FRZ.at[g, j], fss.at[0, g, j], frs.at[0, g, j], Z1
        )

    def f_x(g, j):
        return send(
            FAC.at[4 * g + 2 * (1 - sx) + j, 6:8], FRX.at[g, j], fss.at[1, g, j], frs.at[1, g, j], X1
        )

    def f_c(g, j):
        return send(
            FAC.at[4 * g + 2 * j + 1 - c, 8], FRC.at[g, j], fss.at[2, g, j], frs.at[2, g, j], C1
        )

    def f_y(g, j):
        return send(
            FAC.at[4 * g + 2 * (1 - sy) + j, 9:11], FRY.at[g, j], fss.at[3, g, j], frs.at[3, g, j], Y1
        )

    def pair(fo, fx_, vo, vx):
        lhs = jnp.concatenate(
            [jnp.concatenate([fo[0], fo[1]], axis=1), jnp.concatenate([fx_[1], fx_[0]], axis=1)], axis=0
        )
        res = dot(lhs, jnp.concatenate([vo, vx], axis=0))
        return res[:B], res[B:]

    def one(f, v, w):
        return dot(jnp.concatenate([f[0], f[1]], axis=1), jnp.concatenate([v, w], axis=0))

    def local(i):
        cols = pl.ds(pl.multiple_of(i * WL, WL), WL)
        for k in range(4):
            span = 2**k

            def body(n, carry, k=k, span=span):
                la = lax.div(n, span) * (2 * span) + lax.rem(n, span)
                lb = la + span
                ia = (lax.div(la, 4), lax.rem(lax.div(la, 2), 2), lax.rem(la, 2))
                ib = (lax.div(lb, 4), lax.rem(lax.div(lb, 2), 2), lax.rem(lb, 2))
                va, vb = H[ia[0], ia[1], ia[2], :, cols], H[ib[0], ib[1], ib[2], :, cols]
                oa, ob = pair((FAC[la, k, 0], FAC[la, k, 1]), (FAC[lb, k, 0], FAC[lb, k, 1]), va, vb)
                H[ia[0], ia[1], ia[2], :, cols] = oa
                H[ib[0], ib[1], ib[2], :, cols] = ob
                return carry

            lax.fori_loop(0, 2 * GROUPS, body, 0)

    load_f(4).wait()
    load_f(5).wait()
    scale((4, 5))
    pl.semaphore_wait(barrier, len(partners))
    for j in range(2):
        f_z(0, j).start()
    for k in range(4):
        load_f(k).wait()
    scale((0, 1, 2, 3))
    load_x(0).wait()
    local(0)

    def place(u):
        g, cc = lax.div(u, chunks), lax.rem(u, chunks)
        return g, cc, pl.ds(pl.multiple_of(cc * W, W), W), lax.rem(u, DEPTH)

    def c1(u):
        g, cc, cols, d = place(u)
        return [send(H.at[g, :, 1 - sz, :, cols], R1.at[u], s1.at[d], r1.at[u], Z1)]

    def c2(u):
        d = lax.rem(u, DEPTH)
        return [send(S1.at[d], R2.at[u], s2.at[d], r2.at[u], Z3)]

    def turn(S, R, ss, rs, u, keep, to):
        d = lax.rem(u, DEPTH)
        return [
            send(S.at[d, 1, keep], R.at[u, 0], ss.at[d, 0], rs.at[u, 0], to[0]),
            send(S.at[d, 0, 1 - keep], R.at[u, 1], ss.at[d, 1], rs.at[u, 1], to[1]),
            send(S.at[d, 1, 1 - keep], R.at[u, 2], ss.at[d, 2], rs.at[u, 2], to[2]),
        ]

    kx = sx
    kc = lax.rem(c + sz, 2)
    ky = lax.rem(sx + sy, 2)

    def c3(u):
        return turn(S2, R3, s3, r3, u, kx, (Z1, X1, ZX))

    def c4(u):
        d = lax.rem(u, DEPTH)
        return [send(S3.at[d], R4.at[u], s4.at[d], r4.at[u], X3)]

    def c5(u):
        return turn(S4, R5, s5, r5, u, kc, (X1, C1, XC))

    def c6(u):
        return turn(S5, R6, s6, r6, u, ky, (C1, Y1, YC))

    def c7(u):
        d = lax.rem(u, DEPTH)
        return [send(S6.at[d], R7.at[u], s7.at[d], r7.at[u], Y3)]

    def b0(i):
        return c if i == 0 else 1 - c

    def c8(u):
        g, cc, cols, d = place(u)
        return [
            send(S7.at[d, 1, i], out.at[g, sy, b0(i), :, cols], s8.at[d, i], r8.at[u, i], Y1)
            for i in range(2)
        ]

    def co(u):
        g, cc, cols, d = place(u)
        return [
            pltpu.make_async_copy(S7.at[d, 0, i], out.at[g, sy, b0(i), :, cols], os.at[d, i])
            for i in range(2)
        ]

    def start(copies):
        for copy in copies:
            copy.start()

    def received(copies):
        for copy in copies:
            copy.wait_recv()

    def reuse(u, make):
        @pl.when(u >= DEPTH)
        def _():
            for copy in make(u):
                copy.wait_send()

    def factors_in(u, make):
        g, cc = lax.div(u, chunks), lax.rem(u, chunks)

        @pl.when(cc == 0)
        def _():
            for j in range(2):
                make(g, j).wait_recv()

    def exchange(u, Sin, Rin, Sout, own, oth):
        d = lax.rem(u, DEPTH)
        for i in range(2):
            fo, fx_ = own(i), oth(i)
            Sout[d, 0, i] = one(fo, Sin[d, 0, i], Rin[u, 1, i])
            Sout[d, 1, i] = one(fx_, Sin[d, 1, i], Rin[u, 0, i])

    def both(u, Sin, keep, Rin, first, Sout, own, oth):
        d = lax.rem(u, DEPTH)
        a, b = pair(own(0), oth(0), Sin[d, 0, keep], Rin[u, 1])
        Sout[d, 0, 0] = a
        Sout[d, 1, 0] = b
        a, b = pair(own(1), oth(1), Rin[u, 0], Rin[u, 2])
        Sout[d, 0, 1] = a
        Sout[d, 1, 1] = b

    def stage_z0(u):
        g, cc, cols, d = place(u)
        factors_in(u, f_z)
        reuse(u, c2)
        received(c1(u))
        for j in range(2):
            l = 4 * g + 2 * j + sz
            a, b = pair(
                (FAC[l, 4, 0], FAC[l, 4, 1]), (FRZ[g, j, 0, 0], FRZ[g, j, 0, 1]),
                H[g, j, sz, :, cols], R1[u, j],
            )
            S1[d, 0, j] = a
            S1[d, 1, j] = b
        start(c2(u))

    def stage_z1(u):
        g = lax.div(u, chunks)
        reuse(u, c3)
        received(c2(u))
        exchange(
            u, S1, R2, S2,
            lambda j: (FAC[4 * g + 2 * j + sz, 5, 0], FAC[4 * g + 2 * j + sz, 5, 1]),
            lambda j: (FRZ[g, j, 1, 0], FRZ[g, j, 1, 1]),
        )
        start(c3(u))

    def z_of(i):
        return sz if i == 0 else 1 - sz

    def stage_x0(u):
        g = lax.div(u, chunks)
        factors_in(u, f_x)
        reuse(u, c4)
        received(c3(u))
        both(
            u, S2, kx, R3, sz, S3,
            lambda i: (FAC[4 * g + 2 * sx + z_of(i), 6, 0], FAC[4 * g + 2 * sx + z_of(i), 6, 1]),
            lambda i: (FRX[g, z_of(i), 0, 0], FRX[g, z_of(i), 0, 1]),
        )
        start(c4(u))

    def stage_x1(u):
        g = lax.div(u, chunks)
        reuse(u, c5)
        received(c4(u))
        exchange(
            u, S3, R4, S4,
            lambda i: (FAC[4 * g + 2 * sx + z_of(i), 7, 0], FAC[4 * g + 2 * sx + z_of(i), 7, 1]),
            lambda i: (FRX[g, z_of(i), 1, 0], FRX[g, z_of(i), 1, 1]),
        )
        start(c5(u))

    def x_of(i):
        return sx if i == 0 else 1 - sx

    def stage_c(u):
        g = lax.div(u, chunks)
        factors_in(u, f_c)
        reuse(u, c6)
        received(c5(u))
        both(
            u, S4, kc, R5, sx, S5,
            lambda i: (FAC[4 * g + 2 * x_of(i) + c, 8, 0], FAC[4 * g + 2 * x_of(i) + c, 8, 1]),
            lambda i: (FRC[g, x_of(i), 0], FRC[g, x_of(i), 1]),
        )
        start(c6(u))

    def stage_y0(u):
        g = lax.div(u, chunks)
        factors_in(u, f_y)
        reuse(u, c7)
        received(c6(u))
        both(
            u, S5, ky, R6, c, S6,
            lambda i: (FAC[4 * g + 2 * sy + b0(i), 9, 0], FAC[4 * g + 2 * sy + b0(i), 9, 1]),
            lambda i: (FRY[g, b0(i), 0, 0], FRY[g, b0(i), 0, 1]),
        )
        start(c7(u))

    def stage_y1(u):
        g = lax.div(u, chunks)
        reuse(u, c8)

        @pl.when(u >= DEPTH)
        def _():
            for copy in co(u):
                copy.wait()

        received(c7(u))
        exchange(
            u, S6, R7, S7,
            lambda i: (FAC[4 * g + 2 * sy + b0(i), 10, 0], FAC[4 * g + 2 * sy + b0(i), 10, 1]),
            lambda i: (FRY[g, b0(i), 1, 0], FRY[g, b0(i), 1, 1]),
        )
        start(c8(u))
        start(co(u))

    def stage_swap(u):
        reuse(u, c1)
        start(c1(u))
        g, cc = lax.div(u, chunks), lax.rem(u, chunks)

        @pl.when(jnp.logical_and(g < GROUPS - 1, lax.rem(cc, 4) == 1))
        def _():
            f_z(g + 1, lax.div(cc, 4)).start()

    stages = (stage_swap, stage_z0, stage_z1, stage_x0, stage_x1, stage_c, stage_y0, stage_y1)

    def step(t, carry):
        for off, stage in zip(OFF, stages):
            @pl.when(jnp.logical_and(t >= off, t < off + units))
            def _(off=off, stage=stage):
                stage(t - off)

            if stage is stage_swap:
                @pl.when(jnp.logical_and(t < 2 * (width // WL - 1), lax.rem(t, 2) == 0))
                def _():
                    i = lax.div(t, 2) + 1
                    load_x(i).wait()
                    local(i)

                @pl.when(t == 1)
                def _():
                    for k in (6, 7, 8, 9, 10):
                        load_f(k).wait()
                    scale((6, 7, 8, 9, 10))
                    for g in range(GROUPS):
                        for j in range(2):
                            f_x(g, j).start()
                            f_c(g, j).start()
                            f_y(g, j).start()

        return carry

    lax.fori_loop(0, units + OFF[-1], step, 0)

    for u in range(units - DEPTH, units):
        for make in (c1, c2, c3, c4, c5, c6, c7, c8):
            for copy in make(u):
                copy.wait_send()
        for copy in co(u):
            copy.wait()

    def finish(u, carry):
        received(c8(u))
        return carry

    lax.fori_loop(0, units, finish, 0)
    for g in range(GROUPS):
        for j in range(2):
            for make in (f_z, f_x, f_c, f_y):
                make(g, j).wait_send()


def on_device(x_blocks, factors, pattern):
    blocks, order, width = x_blocks.shape[2:]
    levels = factors.shape[3]
    units = GROUPS * (width // W)
    dma = pltpu.SemaphoreType.DMA
    bf = jnp.bfloat16
    tile = (order, W)
    scratch = [
        pltpu.VMEM((GROUPS, 2, 2, order, width), bf),
        pltpu.VMEM((blocks, levels, 2, order, order), bf),
        pltpu.VMEM((GROUPS, 2, 2, 2, order, order), bf),
        pltpu.VMEM((GROUPS, 2, 2, 2, order, order), bf),
        pltpu.VMEM((GROUPS, 2, 2, order, order), bf),
        pltpu.VMEM((GROUPS, 2, 2, 2, order, order), bf),
        pltpu.VMEM((units, 2) + tile, bf),
        pltpu.VMEM((units, 2, 2) + tile, bf),
        pltpu.VMEM((units, 3) + tile, bf),
        pltpu.VMEM((units, 2, 2) + tile, bf),
        pltpu.VMEM((units, 3) + tile, bf),
        pltpu.VMEM((units, 3) + tile, bf),
        pltpu.VMEM((units, 2, 2) + tile, bf),
    ]
    scratch += [pltpu.VMEM((DEPTH, 2, 2) + tile, bf)] * 7
    scratch += [
        dma((width // WL,)), dma((levels,)), dma((4, GROUPS, 2)), dma((4, GROUPS, 2)),
        dma((units,)), dma((units,)), dma((units, 3)), dma((units,)), dma((units, 3)), dma((units, 3)),
        dma((units,)), dma((units, 2)),
        dma((DEPTH,)), dma((DEPTH,)), dma((DEPTH, 3)), dma((DEPTH,)), dma((DEPTH, 3)), dma((DEPTH, 3)),
        dma((DEPTH,)), dma((DEPTH, 2)), dma((DEPTH, 2)),
    ]
    result = pl.pallas_call(
        kernel,
        out_shape=jax.ShapeDtypeStruct((GROUPS, 2, 2, order, width), bf),
        in_specs=[
            pl.BlockSpec(memory_space=pltpu.SMEM),
            pl.BlockSpec(memory_space=pl.ANY),
            pl.BlockSpec(memory_space=pl.ANY),
        ],
        out_specs=pl.BlockSpec(memory_space=pl.ANY),
        scratch_shapes=scratch,
        name="butterfly",
        cost_estimate=pl.CostEstimate(
            flops=blocks * levels * 4 * order * order * width,
            bytes_accessed=2 * (2 * x_blocks.size + factors.size),
            transcendentals=0,
        ),
        compiler_params=pltpu.CompilerParams(
            collective_id=0, has_side_effects=True, vmem_limit_bytes=60 * 2**20
        ),
    )(
        pattern,
        x_blocks.reshape(GROUPS, 2, 2, order, width),
        factors.reshape(blocks, levels, 2, order, order),
    )
    return result.reshape(1, 1, blocks, order, width)


def solution(mesh):
    return jax.shard_map(
        on_device,
        mesh=mesh,
        in_specs=(
            P("row", "col", None, None, None),
            P("row", "col", None, None, None, None, None),
            P("row", "col", None, None),
        ),
        out_specs=P("row", "col", None, None, None),
        check_vma=False,
    )
```

time: 636 us -> 183 us (0.29)
  waiting for transfers between devices: 534 us -> 0 us
  Pallas kernels: 0 us -> 177 us
  matrix products: 44.3 us -> 0 us
  local copies, waits for them, and re-layouts: 38.1 us -> 6.17 us
  starting transfers between devices: 18.6 us -> 0 us
    ppermute x7 -> x0, waiting for transfers between devices: 534 us -> none  [swapped(): return lax.ppermute(value, axis, pairs)]
    pallas_call x0 -> x1, Pallas kernels: none -> 177 us  [on_device(): pl.pallas_call(kernel, out_shape=jax.ShapeDtypeStruct((GROUPS, 2, 2, orde...]
    dot_general x22 -> x0, matrix products: 44.3 us -> none  [the longest x11 23.1 us: combine(): jnp.einsum('nij,njr->nir', level_w[:, 1], partner, preferred_element_type...]
    rev x4 -> x0, local copies, waits for them, and re-layouts: 18.6 us -> none  [flipped(): array.reshape((count >> bit + 1, 2, 1 << bit) + array.shape[1:])[:, ::-1]]
    ppermute x7 -> x0, starting transfers between devices: 18.6 us -> none  [swapped(): return lax.ppermute(value, axis, pairs)]
    reshape x1 -> x0, local copies, waits for them, and re-layouts: 6.39 us -> none  [on_device(): return current.reshape(1, 1, blocks, order, width)]
  transfers between devices with their start and end apart: 7 -> 0, of which waited for: 7 -> 0; matrix products, arithmetic and copies ran while one was open for 1% -> 0% of each run, Pallas kernels for 0% -> 0%
where the time goes in v1:
time: 183 us
  Pallas kernels  177 us (97%)
  local copies, waits for them, and re-layouts  6.17 us (3%)
    pallas_call x1, Pallas kernels, on_device(): pl.pallas_call(kernel, out_shape=jax.ShapeDtypeStruct((GROUPS, 2, 2, orde...  177 us
    unnamed x2, local copies, waits for them, and re-layouts  6.17 us

profile of v1, /device:TPU:1, one launch (start us, length us, event | category | flops | bytes accessed | tf_op | source)
XLA Modules:
  0.0 182.7 jit_solution(6227373341352160588)
XLA Ops:
  0.0 1.4 copy.4.pat
  1.4 176.6 %butterfly.1 = bf16[4,2,2,128,1024]{4,3,2,1,0:T(8,128)(2,1)} custom-call(s32[1,1,16,11]{3,2,1,0:T(8,128)} %copy.4.pat, bf16[4,2,2,128,1024]{4,3,2,1,0:T(8,128)(2,1)} %bitcast.5, bf16[16,11,2,128,128]{4,3,2,1,0:T(8,128)(2,1)} %bitcast.4), custom_call_target="tpu_custom_call" | custom-call | flops 11811160064 | bytes 19922944 | tf_op jit(solution)/shard_map/butterfly/pallas_call | solution.py:432
  177.9 4.8 %copy.6 = bf16[1,1,16,128,1024]{4,3,2,1,0:T(8,128)(2,1)} copy(bf16[1,1,16,128,1024]{4,3,2,1,0:T(8,128)(2,1)} %bitcast.3) | data formatting | bytes 8388608

commit v2 on v0

v2 whole, which is shorter than its diff:
```python
import functools

import jax
import jax.numpy as jnp
from jax import lax
from jax.experimental import pallas as pl
from jax.experimental.pallas import tpu as pltpu
from jax.sharding import PartitionSpec as P

MESH = pl.DeviceIdType.MESH
B = 128
W = 128
WL = 256
RING = 4
BLOCKS = 16
GROUPS = BLOCKS // RING
DEPTH = 4
OFF = (0, 2, 4, 6, 8, 10)
ORDER = (0, 1, 2, 3, 4, 5)


def dot(lhs, rhs):
    return jnp.dot(lhs, rhs, preferred_element_type=jnp.float32).astype(jnp.bfloat16)


def pair(fa, fb, va, vb):
    lhs = jnp.concatenate(
        [jnp.concatenate([fa[0], fa[1]], axis=1), jnp.concatenate([fb[1], fb[0]], axis=1)], axis=0
    )
    res = dot(lhs, jnp.concatenate([va, vb], axis=0))
    return res[:B], res[B:]


def kernel(
    pat, x_hbm, f_hbm, out, H, FAC, FRZ, FRX, FRC, FRY,
    RZ, HZ, RX, RC, RY, SZ, SX, SC, SY,
    xs, fs, frs, fss,
    rz, rh, rx, rc, ry, ro, sh, sz, shx, sx, sc, sy, os,
):
    width = H.shape[2]
    chunks = width // W
    units = GROUPS * chunks
    row = lax.axis_index("row")
    col = lax.axis_index("col")
    y, c = lax.div(row, 2), lax.rem(row, 2)
    x, z = lax.div(col, 4), lax.rem(col, 4)

    def dev(z_, x_, y_, c_):
        return (y_ * 2 + c_, x_ * 4 + z_)

    def far(p, k):
        return lax.rem(p + k, RING)

    HOPS = (2, 1, 3)

    def send(src, dst, ssem, rsem, to):
        return pltpu.make_async_remote_copy(
            src_ref=src, dst_ref=dst, send_sem=ssem, recv_sem=rsem, device_id=to, device_id_type=MESH
        )

    def load_f(k):
        return pltpu.make_async_copy(f_hbm.at[:, k], FAC.at[:, k], fs.at[k])

    def load_fz(g, n):
        part = pl.ds(RING * g, RING * n)
        return pltpu.make_async_copy(
            f_hbm.at[part, 4:6], FAC.at[part, 4:6], fs.at[4 if g == 0 else 5]
        )

    def load_x(i):
        cols = pl.ds(i * WL, WL)
        return pltpu.make_async_copy(x_hbm.at[:, :, cols], H.at[:, :, cols], xs.at[i])

    load_fz(0, 1).start()
    load_x(0).start()
    for k in range(4):
        load_f(k).start()
    load_fz(1, GROUPS - 1).start()
    for i in range(1, width // WL):
        load_x(i).start()
    for k in range(6, 11):
        load_f(k).start()

    barrier = pltpu.get_barrier_semaphore()
    partners = [dev(far(z, k), x, y, c) for k in HOPS]
    partners += [dev(z, far(x, k), y, e) for k in HOPS for e in (c, 1 - c)]
    partners += [dev(z, x, far(y, k), e) for k in HOPS for e in (c, 1 - c)]
    partners += [dev(z, x, y, 1 - c)]
    for to in partners:
        pl.semaphore_signal(barrier, inc=1, device_id=to, device_id_type=MESH)

    def scale(first, count, levels):
        def body(l, carry):
            for k in levels:
                m = pat[0, k, 0, l].astype(jnp.float32)
                FAC[l, k, 1] = (FAC[l, k, 1].astype(jnp.float32) * m).astype(jnp.bfloat16)
            return carry

        lax.fori_loop(first, first + count, body, 0)

    def f_z(g, k, n):
        q = far(z, k)
        return send(
            FAC.at[RING * g + q, 4 + n], FRZ.at[g, z, n], fss.at[0, g, k, n], frs.at[0, g, z, n],
            dev(q, x, y, c),
        )

    def f_z_in(g, k, n):
        p = far(z, k)
        return send(
            FAC.at[RING * g + p, 4 + n], FRZ.at[g, p, n], fss.at[0, g, k, n], frs.at[0, g, p, n],
            dev(p, x, y, c),
        )

    def f_x(g, k):
        q = far(x, k)
        return send(
            FAC.at[RING * g + q, 6:8], FRX.at[g, x], fss.at[1, g, k, 0], frs.at[1, g, x, 0], dev(z, q, y, c)
        )

    def f_x_in(g, k):
        p = far(x, k)
        return send(
            FAC.at[RING * g + p, 6:8], FRX.at[g, p], fss.at[1, g, k, 0], frs.at[1, g, p, 0], dev(z, p, y, c)
        )

    def f_y(g, k):
        q = far(y, k)
        return send(
            FAC.at[RING * g + q, 9:11], FRY.at[g, y], fss.at[2, g, k, 0], frs.at[2, g, y, 0], dev(z, x, q, c)
        )

    def f_y_in(g, k):
        p = far(y, k)
        return send(
            FAC.at[RING * g + p, 9:11], FRY.at[g, p], fss.at[2, g, k, 0], frs.at[2, g, p, 0], dev(z, x, p, c)
        )

    def f_c(g, j):
        return send(
            FAC.at[RING * g + 2 * j + 1 - c, 8], FRC.at[g, j, c],
            fss.at[3, g, j, 0], frs.at[3, g, j, 0], dev(z, x, y, 1 - c),
        )

    def f_c_in(g, j):
        return send(
            FAC.at[RING * g + 2 * j + 1 - c, 8], FRC.at[g, j, 1 - c],
            fss.at[3, g, j, 0], frs.at[3, g, j, 0], dev(z, x, y, 1 - c),
        )

    def local(i):
        cols = pl.ds(pl.multiple_of(i * WL, WL), WL)
        for k in range(4):
            span = 2**k
            places = []
            for n in range(BLOCKS // 2):
                la = n // span * (2 * span) + n % span
                places.append((la, la + span))
            results = []
            for la, lb in places:
                results.append(
                    pair(
                        (FAC[la, k, 0], FAC[la, k, 1]), (FAC[lb, k, 0], FAC[lb, k, 1]),
                        H[la, :, cols], H[lb, :, cols],
                    )
                )
            for (la, lb), (oa, ob) in zip(places, results):
                H[la, :, cols] = oa
                H[lb, :, cols] = ob

    load_fz(0, 1).wait()
    scale(0, RING, (4, 5))
    pl.semaphore_wait(barrier, len(partners))
    for n in range(2):
        for k in HOPS:
            f_z(0, k, n).start()
    for k in range(4):
        load_f(k).wait()
    scale(0, BLOCKS, (0, 1, 2, 3))
    load_x(0).wait()
    local(0)

    def place(u):
        g, cc = lax.div(u, chunks), lax.rem(u, chunks)
        return g, pl.ds(pl.multiple_of(cc * W, W), W), lax.rem(u, DEPTH)

    def z_out(u, k):
        g, cols, d = place(u)
        q = far(z, k)
        return send(
            H.at[RING * g + q, :, cols], RZ.at[u, z], sh.at[d, k], rz.at[u, z], dev(q, x, y, c)
        )

    def z_out_in(u, k):
        p = far(z, k)
        return send(SZ.at[0, p], RZ.at[u, p], sh.at[0, k], rz.at[u, p], dev(p, x, y, c))

    def z_back(u, k):
        d = lax.rem(u, DEPTH)
        p = far(z, k)
        return send(SZ.at[d, p], HZ.at[u, z], sz.at[d, k], rh.at[u, z], dev(p, x, y, c))

    def z_back_in(u, k):
        p = far(z, k)
        return send(SZ.at[0, p], HZ.at[u, p], sz.at[0, k], rh.at[u, p], dev(p, x, y, c))

    def x_out(u, k):
        d = lax.rem(u, DEPTH)
        q = far(x, k)
        return send(HZ.at[u, q], RX.at[u, x], shx.at[d, k], rx.at[u, x], dev(z, q, y, c))

    def x_out_in(u, k):
        p = far(x, k)
        return send(SX.at[0, p], RX.at[u, p], shx.at[0, k], rx.at[u, p], dev(z, p, y, c))

    cx = lax.rem(x, 2)
    cy = lax.rem(y, 2)

    def x_back(u, k):
        d = lax.rem(u, DEPTH)
        p = far(x, k)
        return send(
            SX.at[d, p], RC.at[u, lax.div(x, 2), c], sx.at[d, k], rc.at[u, lax.div(x, 2), c],
            dev(z, p, y, cx),
        )

    def x_back_in(u, j, e):
        return send(
            SX.at[0, 0], RC.at[u, j, e], sx.at[0, 0], rc.at[u, j, e], dev(z, c + 2 * j, y, e)
        )

    def y_out(u, j, e):
        d = lax.rem(u, DEPTH)
        to = c if e == 0 else 1 - c
        return send(
            SC.at[d, j, to], RY.at[u, y], sc.at[d, j, e], ry.at[u, y], dev(z, x, c + 2 * j, to)
        )

    def y_out_in(u, k):
        p = far(y, k)
        return send(SY.at[0, p], RY.at[u, p], sc.at[0, 0, 0], ry.at[u, p], dev(z, x, p, cy))

    def y_back(u, k):
        g, cols, d = place(u)
        p = far(y, k)
        return send(
            SY.at[d, p], out.at[RING * g + y, :, cols], sy.at[d, k], ro.at[u, y], dev(z, x, p, c)
        )

    def y_back_in(u, k):
        g, cols, d = place(u)
        p = far(y, k)
        return send(
            SY.at[0, p], out.at[RING * g + p, :, cols], sy.at[0, k], ro.at[u, p], dev(z, x, p, c)
        )

    def keep(u):
        g, cols, d = place(u)
        return pltpu.make_async_copy(SY.at[d, y], out.at[RING * g + y, :, cols], os.at[d])

    def reuse(u, waits):
        @pl.when(u >= DEPTH)
        def _():
            waits(u)

    def sent(copy):
        return lambda u: [copy(u, k).wait_send() for k in HOPS]

    def x_back_sent(u):
        for k in HOPS:
            x_back(u, k).wait_send()

        @pl.when(cx != c)
        def _():
            x_back(u, 0).wait_send()

    def y_out_sent(u):
        for j in range(2):
            y_out(u, j, 1).wait_send()

            @pl.when(y != c + 2 * j)
            def _():
                y_out(u, j, 0).wait_send()

    def y_back_sent(u):
        for k in HOPS:
            y_back(u, k).wait_send()
        keep(u).wait()

    def first_chunk(u, wait):
        g, cc = lax.div(u, chunks), lax.rem(u, chunks)

        @pl.when(cc == 0)
        def _():
            wait(g)

    def two_levels(F, g, R, u):
        v = [R[u, p] for p in range(RING)]
        for level, pairs in enumerate((((0, 1), (2, 3)), ((0, 2), (1, 3)))):
            for a, b in pairs:
                v[a], v[b] = pair(
                    (F[g, a, level, 0], F[g, a, level, 1]), (F[g, b, level, 0], F[g, b, level, 1]),
                    v[a], v[b],
                )
        return v

    def stage_z_out(u):
        reuse(u, sent(z_out))
        for k in HOPS:
            z_out(u, k).start()
        g, cols, d = place(u)
        RZ[u, z] = H[RING * g + z, :, cols]
        cc = lax.rem(u, chunks)
        for i, k in enumerate(HOPS):
            for n in range(2):
                @pl.when(jnp.logical_and(g < GROUPS - 1, cc == 3 * n + i + 1))
                def _(k=k, n=n):
                    f_z(g + 1, k, n).start()

            @pl.when(jnp.logical_and(jnp.logical_and(g > 0, g < GROUPS - 1), cc == 2 * i))
            def _(k=k):
                f_x(g + 1, k).start()

    def stage_z(u):
        g, cols, d = place(u)
        first_chunk(u, lambda g: [f_z_in(g, k, n).wait_recv() for k in HOPS for n in range(2)])
        reuse(u, sent(z_back))
        for k in HOPS:
            z_out_in(u, k).wait_recv()
        v = two_levels(FRZ, g, RZ, u)
        for p in range(RING):
            SZ[d, p] = v[p]
        for k in HOPS:
            z_back(u, k).start()
        HZ[u, z] = SZ[d, z]

    def stage_x_out(u):
        reuse(u, sent(x_out))
        for k in HOPS:
            z_back_in(u, k).wait_recv()
        for k in HOPS:
            x_out(u, k).start()
        RX[u, x] = HZ[u, x]

    def stage_x(u):
        g, cols, d = place(u)
        first_chunk(u, lambda g: [f_x_in(g, k).wait_recv() for k in HOPS])
        reuse(u, x_back_sent)
        for k in HOPS:
            x_out_in(u, k).wait_recv()
        v = two_levels(FRX, g, RX, u)
        for p in range(RING):
            SX[d, p] = v[p]
        for k in HOPS:
            x_back(u, k).start()

        @pl.when(cx != c)
        def _():
            x_back(u, 0).start()

        @pl.when(cx == c)
        def _():
            RC[u, lax.div(x, 2), c] = SX[d, x]

    def stage_c(u):
        g, cols, d = place(u)
        first_chunk(u, lambda g: [f_c_in(g, j).wait_recv() for j in range(2)])
        reuse(u, y_out_sent)
        for j in range(2):
            x_back_in(u, j, 1 - c).wait_recv()

            @pl.when(x != c + 2 * j)
            def _():
                x_back_in(u, j, c).wait_recv()

        for j in range(2):
            a, b = pair(
                (FRC[g, j, 0, 0], FRC[g, j, 0, 1]), (FRC[g, j, 1, 0], FRC[g, j, 1, 1]),
                RC[u, j, 0], RC[u, j, 1],
            )
            SC[d, j, 0] = a
            SC[d, j, 1] = b
        for j in range(2):
            y_out(u, j, 1).start()

            @pl.when(y != c + 2 * j)
            def _():
                y_out(u, j, 0).start()

            @pl.when(y == c + 2 * j)
            def _():
                RY[u, y] = SC[d, j, c]

    def stage_y(u):
        g, cols, d = place(u)
        first_chunk(u, lambda g: [f_y_in(g, k).wait_recv() for k in HOPS])
        reuse(u, y_back_sent)
        for k in HOPS:
            y_out_in(u, k).wait_recv()

        @pl.when(cy != c)
        def _():
            y_out_in(u, 0).wait_recv()

        v = two_levels(FRY, g, RY, u)
        for p in range(RING):
            SY[d, p] = v[p]
        for k in HOPS:
            y_back(u, k).start()
        keep(u).start()

    stages = (stage_z_out, stage_z, stage_x_out, stage_x, stage_c, stage_y)

    def own_factors(g, carry):
        FRX[g, x] = FAC[RING * g + x, 6:8]
        FRY[g, y] = FAC[RING * g + y, 9:11]
        for j in range(2):
            FRC[g, j, c] = FAC[RING * g + 2 * j + c, 8]
        return carry

    def own_z(g, carry):
        FRZ[g, z] = FAC[RING * g + z, 4:6]
        return carry

    own_z(0, 0)

    def step(t, carry):
        for n in ORDER:
            off, stage = OFF[n], stages[n]

            @pl.when(jnp.logical_and(t >= off, t < off + units))
            def _(off=off, stage=stage):
                stage(t - off)

            if stage is stage_z_out:
                @pl.when(t == 0)
                def _():
                    load_fz(1, GROUPS - 1).wait()
                    scale(RING, BLOCKS - RING, (4, 5))
                    lax.fori_loop(1, GROUPS, own_z, 0)

                @pl.when(jnp.logical_and(t < 2 * (width // WL - 1), lax.rem(t, 2) == 0))
                def _():
                    i = lax.div(t, 2) + 1
                    load_x(i).wait()
                    local(i)

                @pl.when(t == 1)
                def _():
                    for k in range(6, 11):
                        load_f(k).wait()
                    scale(0, BLOCKS, (6, 7, 8, 9, 10))
                    for g in range(GROUPS):
                        for k in HOPS if g < 2 else ():
                            f_x(g, k).start()
                        for j in range(2):
                            f_c(g, j).start()
                        for k in HOPS:
                            f_y(g, k).start()
                    lax.fori_loop(0, GROUPS, own_factors, 0)

        return carry

    lax.fori_loop(0, units + max(OFF), step, 0)

    def last(u, carry):
        for copy in (z_out, z_back, x_out):
            sent(copy)(u)
        x_back_sent(u)
        y_out_sent(u)
        y_back_sent(u)
        return carry

    lax.fori_loop(units - DEPTH, units, last, 0)

    def finish(u, carry):
        for k in HOPS:
            y_back_in(u, k).wait_recv()
        return carry

    lax.fori_loop(0, units, finish, 0)
    for g in range(GROUPS):
        for k in HOPS:
            f_x(g, k).wait_send()
            f_y(g, k).wait_send()
            for n in range(2):
                f_z(g, k, n).wait_send()
        for j in range(2):
            f_c(g, j).wait_send()


def on_device(x_blocks, factors, pattern):
    blocks, order, width = x_blocks.shape[2:]
    levels = factors.shape[3]
    units = GROUPS * (width // W)
    dma = pltpu.SemaphoreType.DMA
    bf = jnp.bfloat16
    tile = (order, W)
    square = (order, order)
    scratch = [
        pltpu.VMEM((blocks, order, width), bf),
        pltpu.VMEM((blocks, levels, 2) + square, bf),
        pltpu.VMEM((GROUPS, RING, 2, 2) + square, bf),
        pltpu.VMEM((GROUPS, RING, 2, 2) + square, bf),
        pltpu.VMEM((GROUPS, 2, 2, 2) + square, bf),
        pltpu.VMEM((GROUPS, RING, 2, 2) + square, bf),
    ]
    scratch += [pltpu.VMEM((units, RING) + tile, bf)] * 3
    scratch += [pltpu.VMEM((units, 2, 2) + tile, bf), pltpu.VMEM((units, RING) + tile, bf)]
    scratch += [pltpu.VMEM((DEPTH, RING) + tile, bf)] * 2
    scratch += [pltpu.VMEM((DEPTH, 2, 2) + tile, bf), pltpu.VMEM((DEPTH, RING) + tile, bf)]
    scratch += [
        dma((width // WL,)), dma((levels,)), dma((4, GROUPS, RING, 2)), dma((4, GROUPS, RING, 2)),
        dma((units, RING)), dma((units, RING)), dma((units, RING)), dma((units, 2, 2)),
        dma((units, RING)), dma((units, RING)),
        dma((DEPTH, RING)), dma((DEPTH, RING)), dma((DEPTH, RING)), dma((DEPTH, RING)),
        dma((DEPTH, 2, 2)), dma((DEPTH, RING)), dma((DEPTH,)),
    ]
    result = pl.pallas_call(
        kernel,
        out_shape=jax.ShapeDtypeStruct((blocks, order, width), bf),
        in_specs=[
            pl.BlockSpec(memory_space=pltpu.SMEM),
            pl.BlockSpec(memory_space=pl.ANY),
            pl.BlockSpec(memory_space=pl.ANY),
        ],
        out_specs=pl.BlockSpec(memory_space=pl.ANY),
        scratch_shapes=scratch,
        name="butterfly",
        cost_estimate=pl.CostEstimate(
            flops=blocks * levels * 4 * order * order * width,
            bytes_accessed=2 * (2 * x_blocks.size + factors.size),
            transcendentals=0,
        ),
        compiler_params=pltpu.CompilerParams(
            collective_id=0, has_side_effects=True, vmem_limit_bytes=48 * 2**20
        ),
    )(
        jnp.transpose(pattern, (0, 3, 1, 2)),
        x_blocks.reshape(blocks, order, width),
        factors.reshape(blocks, levels, 2, order, order),
    )
    return result.reshape(1, 1, blocks, order, width)


def solution(mesh):
    return jax.shard_map(
        on_device,
        mesh=mesh,
        in_specs=(
            P("row", "col", None, None, None),
            P("row", "col", None, None, None, None, None),
            P("row", "col", None, None),
        ),
        out_specs=P("row", "col", None, None, None),
        check_vma=False,
    )
```

time: 636 us -> 160 us (0.25)
  waiting for transfers between devices: 534 us -> 0 us
  Pallas kernels: 0 us -> 157 us
  matrix products: 44.3 us -> 0 us
  local copies, waits for them, and re-layouts: 38.1 us -> 2.71 us
  starting transfers between devices: 18.6 us -> 0 us
    ppermute x7 -> x0, waiting for transfers between devices: 534 us -> none  [swapped(): return lax.ppermute(value, axis, pairs)]
    pallas_call x0 -> x1, Pallas kernels: none -> 157 us  [on_device(): pl.pallas_call(kernel, out_shape=jax.ShapeDtypeStruct((blocks, order, wid...]
    dot_general x22 -> x0, matrix products: 44.3 us -> none  [the longest x11 23.1 us: combine(): jnp.einsum('nij,njr->nir', level_w[:, 1], partner, preferred_element_type...]
    rev x4 -> x0, local copies, waits for them, and re-layouts: 18.6 us -> none  [flipped(): array.reshape((count >> bit + 1, 2, 1 << bit) + array.shape[1:])[:, ::-1]]
    ppermute x7 -> x0, starting transfers between devices: 18.6 us -> none  [swapped(): return lax.ppermute(value, axis, pairs)]
    unnamed x26 -> x3, local copies, waits for them, and re-layouts: 9.35 us -> 2.71 us
    reshape x1 -> x0, local copies, waits for them, and re-layouts: 6.39 us -> none  [on_device(): return current.reshape(1, 1, blocks, order, width)]
  transfers between devices with their start and end apart: 7 -> 0, of which waited for: 7 -> 0; matrix products, arithmetic and copies ran while one was open for 1% -> 0% of each run, Pallas kernels for 0% -> 0%
where the time goes in v2:
time: 160 us
  Pallas kernels  157 us (98%)
  local copies, waits for them, and re-layouts  2.71 us (2%)
    pallas_call x1, Pallas kernels, on_device(): pl.pallas_call(kernel, out_shape=jax.ShapeDtypeStruct((blocks, order, wid...  157 us

profile of v2, /device:TPU:1, one launch (start us, length us, event | category | flops | bytes accessed | tf_op | source)
XLA Modules:
  0.0 160.1 jit_solution(11576251192879349130)
XLA Ops:
  0.0 0.0 copy-start
  0.0 0.7 copy-done
  0.7 157.4 %butterfly.1 = bf16[16,128,1024]{2,1,0:T(8,128)(2,1)S(1)} custom-call(s32[1,11,1,16]{3,2,1,0:T(1,128)S(1)} %bitcast.5, bf16[16,128,1024]{2,1,0:T(8,128)(2,1)} %bitcast.7, bf16[16,11,2,128,128]{4,3,2,1,0:T(8,128)(2,1)} %bitcast.6), custom_call_target="tpu_custom_call" | custom-call | flops 11811160064 | bytes 19922944 | tf_op jit(solution)/shard_map/butterfly/pallas_call | solution.py:519
  158.1 2.0 %copy.5 = bf16[1,1,16,128,1024]{4,3,2,1,0:T(8,128)(2,1)} copy(bf16[1,1,16,128,1024]{4,3,2,1,0:T(8,128)(2,1)S(1)} %bitcast.4) | data formatting | bytes 8388608
Async XLA Ops:
  0.0 0.7 copy-start

commit v3 on v2

v3 whole, which is shorter than its diff:
```python
import functools

import jax
import jax.numpy as jnp
from jax import lax
from jax.experimental import pallas as pl
from jax.experimental.pallas import tpu as pltpu
from jax.sharding import PartitionSpec as P

MESH = pl.DeviceIdType.MESH
B = 128
W = 128
WL = 256
RING = 4
BLOCKS = 16
GROUPS = BLOCKS // RING
OFF = (0, 2, 4, 6, 8, 10)
ORDER = (0, 1, 2, 3, 4, 5)


def dot(lhs, rhs):
    return jnp.dot(lhs, rhs, preferred_element_type=jnp.float32).astype(jnp.bfloat16)


def pair(fa, fb, va, vb):
    lhs = jnp.concatenate(
        [jnp.concatenate([fa[0], fa[1]], axis=1), jnp.concatenate([fb[1], fb[0]], axis=1)], axis=0
    )
    res = dot(lhs, jnp.concatenate([va, vb], axis=0))
    return res[:B], res[B:]


def kernel(
    pat, x_hbm, f_hbm, out, H, FAC, FRZ, FRX, FRC, FRY,
    RZ, HZ, RX, RC, RY,
    xs, fs, frs, fss,
    rz, rh, rx, rc, ry, ro, ss, os,
):
    width = H.shape[2]
    chunks = width // W
    units = GROUPS * chunks
    row = lax.axis_index("row")
    col = lax.axis_index("col")
    y, c = lax.div(row, 2), lax.rem(row, 2)
    x, z = lax.div(col, 4), lax.rem(col, 4)

    def dev(z_, x_, y_, c_):
        return (y_ * 2 + c_, x_ * 4 + z_)

    def far(p, k):
        return lax.rem(p + k, RING)

    HOPS = (2, 1, 3)

    def send(src, dst, ssem, rsem, to):
        return pltpu.make_async_remote_copy(
            src_ref=src, dst_ref=dst, send_sem=ssem, recv_sem=rsem, device_id=to, device_id_type=MESH
        )

    def load_f(k):
        return pltpu.make_async_copy(f_hbm.at[:, k], FAC.at[:, k], fs.at[k])

    def load_fz(g, n):
        part = pl.ds(RING * g, RING * n)
        return pltpu.make_async_copy(
            f_hbm.at[part, 4:6], FAC.at[part, 4:6], fs.at[4 if g == 0 else 5]
        )

    def load_x(i):
        cols = pl.ds(i * WL, WL)
        return pltpu.make_async_copy(x_hbm.at[:, :, cols], H.at[:, :, cols], xs.at[i])

    load_fz(0, 1).start()
    load_x(0).start()
    for k in range(4):
        load_f(k).start()

    barrier = pltpu.get_barrier_semaphore()
    partners = [dev(far(z, k), x, y, c) for k in HOPS]
    partners += [dev(z, far(x, k), y, e) for k in HOPS for e in (c, 1 - c)]
    partners += [dev(z, x, far(y, k), e) for k in HOPS for e in (c, 1 - c)]
    partners += [dev(z, x, y, 1 - c)]
    for to in partners:
        pl.semaphore_signal(barrier, inc=1, device_id=to, device_id_type=MESH)

    def scale(first, count, levels):
        def body(l, carry):
            for k in levels:
                m = pat[0, k, 0, l].astype(jnp.float32)
                FAC[l, k, 1] = (FAC[l, k, 1].astype(jnp.float32) * m).astype(jnp.bfloat16)
            return carry

        lax.fori_loop(first, first + count, body, 0)

    def waits(region, sem):
        return send(region, region, sem, sem, dev(z, x, y, 1 - c))

    def f_z(g, k, n):
        q = far(z, k)
        return send(
            FAC.at[RING * g + q, 4 + n], FRZ.at[g, z, n], fss.at[0], frs.at[0, g], dev(q, x, y, c)
        )

    def f_x(g, k):
        q = far(x, k)
        return send(
            FAC.at[RING * g + q, 6:8], FRX.at[g, x], fss.at[1], frs.at[1, g], dev(z, q, y, c)
        )

    def f_y(g, k):
        q = far(y, k)
        return send(
            FAC.at[RING * g + q, 9:11], FRY.at[g, y], fss.at[2], frs.at[2, g], dev(z, x, q, c)
        )

    def f_c(g, j):
        return send(
            FAC.at[RING * g + 2 * j + 1 - c, 8], FRC.at[g, j, c], fss.at[3], frs.at[3, g],
            dev(z, x, y, 1 - c),
        )

    def local(i):
        cols = pl.ds(pl.multiple_of(i * WL, WL), WL)
        for k in range(4):
            span = 2**k
            places = []
            for n in range(BLOCKS // 2):
                la = n // span * (2 * span) + n % span
                places.append((la, la + span))
            results = []
            for la, lb in places:
                results.append(
                    pair(
                        (FAC[la, k, 0], FAC[la, k, 1]), (FAC[lb, k, 0], FAC[lb, k, 1]),
                        H[la, :, cols], H[lb, :, cols],
                    )
                )
            for (la, lb), (oa, ob) in zip(places, results):
                H[la, :, cols] = oa
                H[lb, :, cols] = ob

    load_fz(0, 1).wait()
    scale(0, RING, (4, 5))
    pl.semaphore_wait(barrier, len(partners))
    for n in range(2):
        for k in HOPS:
            f_z(0, k, n).start()
    for k in range(4):
        load_f(k).wait()
        scale(0, BLOCKS, (k,))
    load_x(0).wait()
    load_fz(1, GROUPS - 1).start()
    for i in range(1, width // WL):
        load_x(i).start()
    for k in range(6, 11):
        load_f(k).start()
    local(0)

    def place(u):
        g, cc = lax.div(u, chunks), lax.rem(u, chunks)
        return g, pl.ds(pl.multiple_of(cc * W, W), W)

    def z_out(u, k):
        g, cols = place(u)
        q = far(z, k)
        return send(H.at[RING * g + q, :, cols], RZ.at[u, z], ss.at[0], rz.at[u], dev(q, x, y, c))

    def z_back(u, k):
        p = far(z, k)
        return send(RZ.at[u, p], HZ.at[u, z], ss.at[1], rh.at[u], dev(p, x, y, c))

    def x_out(u, k):
        q = far(x, k)
        return send(HZ.at[u, q], RX.at[u, x], ss.at[2], rx.at[u], dev(z, q, y, c))

    cx = lax.rem(x, 2)
    cy = lax.rem(y, 2)

    def x_back(u, k):
        p = far(x, k)
        return send(
            RX.at[u, p], RC.at[u, lax.div(x, 2), c], ss.at[3], rc.at[u], dev(z, p, y, cx)
        )

    def y_out(u, j, to):
        return send(RC.at[u, j, to], RY.at[u, y], ss.at[4], ry.at[u], dev(z, x, c + 2 * j, to))

    def y_back(u, k):
        g, cols = place(u)
        p = far(y, k)
        return send(
            RY.at[u, p], out.at[RING * g + y, :, cols], ss.at[5], ro, dev(z, x, p, c)
        )

    def keep(u):
        g, cols = place(u)
        return pltpu.make_async_copy(RY.at[u, y], out.at[RING * g + y, :, cols], os)

    def first_chunk(u, wait):
        g, cc = lax.div(u, chunks), lax.rem(u, chunks)

        @pl.when(cc == 0)
        def _():
            wait(g)

    def two_levels(F, g, R, u):
        v = [R[u, p] for p in range(RING)]
        for level, pairs in enumerate((((0, 1), (2, 3)), ((0, 2), (1, 3)))):
            for a, b in pairs:
                v[a], v[b] = pair(
                    (F[g, a, level, 0], F[g, a, level, 1]), (F[g, b, level, 0], F[g, b, level, 1]),
                    v[a], v[b],
                )
        for p in range(RING):
            R[u, p] = v[p]

    def stage_z_out(u):
        for k in HOPS:
            z_out(u, k).start()
        g, cols = place(u)
        RZ[u, z] = H[RING * g + z, :, cols]
        cc = lax.rem(u, chunks)
        for i, k in enumerate(HOPS):
            for n in range(2):
                @pl.when(jnp.logical_and(g < GROUPS - 1, cc == 3 * n + i + 1))
                def _(k=k, n=n):
                    f_z(g + 1, k, n).start()

            @pl.when(jnp.logical_and(jnp.logical_and(g > 0, g < GROUPS - 1), cc == 2 * i))
            def _(k=k):
                f_x(g + 1, k).start()

    def stage_z(u):
        g, cols = place(u)
        first_chunk(u, lambda g: waits(FRZ.at[g, 0 : RING - 1], frs.at[0, g]).wait_recv())
        waits(RZ.at[u, 0 : RING - 1], rz.at[u]).wait_recv()
        two_levels(FRZ, g, RZ, u)
        for k in HOPS:
            z_back(u, k).start()
        HZ[u, z] = RZ[u, z]

    def stage_x_out(u):
        waits(HZ.at[u, 0 : RING - 1], rh.at[u]).wait_recv()
        for k in HOPS:
            x_out(u, k).start()
        RX[u, x] = HZ[u, x]

    def stage_x(u):
        g, cols = place(u)
        first_chunk(u, lambda g: waits(FRX.at[g, 0 : RING - 1], frs.at[1, g]).wait_recv())
        waits(RX.at[u, 0 : RING - 1], rx.at[u]).wait_recv()
        two_levels(FRX, g, RX, u)
        for k in HOPS:
            x_back(u, k).start()

        @pl.when(cx != c)
        def _():
            x_back(u, 0).start()

        @pl.when(cx == c)
        def _():
            RC[u, lax.div(x, 2), c] = RX[u, x]

    def stage_c(u):
        g, cols = place(u)
        first_chunk(u, lambda g: waits(FRC.at[g, :, 0], frs.at[3, g]).wait_recv())

        @pl.when(cx == c)
        def _():
            waits(RX.at[u, 0 : RING - 1], rc.at[u]).wait_recv()

        @pl.when(cx != c)
        def _():
            waits(RX.at[u], rc.at[u]).wait_recv()

        for j in range(2):
            a, b = pair(
                (FRC[g, j, 0, 0], FRC[g, j, 0, 1]), (FRC[g, j, 1, 0], FRC[g, j, 1, 1]),
                RC[u, j, 0], RC[u, j, 1],
            )
            RC[u, j, 0] = a
            RC[u, j, 1] = b
        for j in range(2):
            y_out(u, j, 1 - c).start()

            @pl.when(y != c + 2 * j)
            def _():
                y_out(u, j, c).start()

            @pl.when(y == c + 2 * j)
            def _():
                RY[u, y] = RC[u, j, c]

    def stage_y(u):
        g, cols = place(u)
        first_chunk(u, lambda g: waits(FRY.at[g, 0 : RING - 1], frs.at[2, g]).wait_recv())

        @pl.when(cy == c)
        def _():
            waits(RY.at[u, 0 : RING - 1], ry.at[u]).wait_recv()

        @pl.when(cy != c)
        def _():
            waits(RY.at[u], ry.at[u]).wait_recv()

        two_levels(FRY, g, RY, u)
        for k in HOPS:
            y_back(u, k).start()
        keep(u).start()

    stages = (stage_z_out, stage_z, stage_x_out, stage_x, stage_c, stage_y)

    def own_factors(g, carry):
        FRX[g, x] = FAC[RING * g + x, 6:8]
        FRY[g, y] = FAC[RING * g + y, 9:11]
        for j in range(2):
            FRC[g, j, c] = FAC[RING * g + 2 * j + c, 8]
        return carry

    def own_z(g, carry):
        FRZ[g, z] = FAC[RING * g + z, 4:6]
        return carry

    own_z(0, 0)

    def step(t, carry):
        for n in ORDER:
            off, stage = OFF[n], stages[n]

            @pl.when(jnp.logical_and(t >= off, t < off + units))
            def _(off=off, stage=stage):
                stage(t - off)

            if stage is stage_z_out:
                @pl.when(t == 0)
                def _():
                    load_fz(1, GROUPS - 1).wait()
                    scale(RING, BLOCKS - RING, (4, 5))
                    lax.fori_loop(1, GROUPS, own_z, 0)

                @pl.when(jnp.logical_and(t < 2 * (width // WL - 1), lax.rem(t, 2) == 0))
                def _():
                    i = lax.div(t, 2) + 1
                    load_x(i).wait()
                    local(i)

                @pl.when(t == 1)
                def _():
                    for k in range(6, 11):
                        load_f(k).wait()
                    scale(0, BLOCKS, (6, 7, 8, 9, 10))
                    for g in range(GROUPS):
                        for k in HOPS if g < 2 else ():
                            f_x(g, k).start()
                        for j in range(2):
                            f_c(g, j).start()
                        for k in HOPS:
                            f_y(g, k).start()
                    lax.fori_loop(0, GROUPS, own_factors, 0)

        return carry

    lax.fori_loop(0, units + max(OFF), step, 0)

    own = RING - 1
    waits(out.at[0 : own * GROUPS], ro).wait_recv()
    pltpu.make_async_copy(out.at[0:GROUPS], out.at[0:GROUPS], os).wait()
    for n, R in enumerate((RZ, RZ, RZ)):
        waits(R.at[:, 0:own], ss.at[n]).wait_send()
    waits(RY.at[:, 0:own], ss.at[5]).wait_send()

    @pl.when(cx == c)
    def _():
        waits(RX.at[:, 0:own], ss.at[3]).wait_send()

    @pl.when(cx != c)
    def _():
        waits(RX, ss.at[3]).wait_send()

    @pl.when(cy == c)
    def _():
        waits(RX.at[:, 0:own], ss.at[4]).wait_send()

    @pl.when(cy != c)
    def _():
        waits(RX, ss.at[4]).wait_send()

    for n, F in enumerate((FRZ, FRX, FRY)):
        waits(F.at[:, 0:own], fss.at[n]).wait_send()
    waits(FRC.at[:, :, 0], fss.at[3]).wait_send()


def on_device(x_blocks, factors, pattern):
    blocks, order, width = x_blocks.shape[2:]
    levels = factors.shape[3]
    units = GROUPS * (width // W)
    dma = pltpu.SemaphoreType.DMA
    bf = jnp.bfloat16
    tile = (order, W)
    square = (order, order)
    scratch = [
        pltpu.VMEM((blocks, order, width), bf),
        pltpu.VMEM((blocks, levels, 2) + square, bf),
        pltpu.VMEM((GROUPS, RING, 2, 2) + square, bf),
        pltpu.VMEM((GROUPS, RING, 2, 2) + square, bf),
        pltpu.VMEM((GROUPS, 2, 2, 2) + square, bf),
        pltpu.VMEM((GROUPS, RING, 2, 2) + square, bf),
    ]
    scratch += [pltpu.VMEM((units, RING) + tile, bf)] * 3
    scratch += [pltpu.VMEM((units, 2, 2) + tile, bf), pltpu.VMEM((units, RING) + tile, bf)]
    scratch += [
        dma((width // WL,)), dma((levels,)), dma((4, GROUPS)), dma((4,)),
        dma((units,)), dma((units,)), dma((units,)), dma((units,)), dma((units,)), dma, dma((6,)), dma,
    ]
    result = pl.pallas_call(
        kernel,
        out_shape=jax.ShapeDtypeStruct((blocks, order, width), bf),
        in_specs=[
            pl.BlockSpec(memory_space=pltpu.SMEM),
            pl.BlockSpec(memory_space=pl.ANY),
            pl.BlockSpec(memory_space=pl.ANY),
        ],
        out_specs=pl.BlockSpec(memory_space=pl.ANY),
        scratch_shapes=scratch,
        name="butterfly",
        cost_estimate=pl.CostEstimate(
            flops=blocks * levels * 4 * order * order * width,
            bytes_accessed=2 * (2 * x_blocks.size + factors.size),
            transcendentals=0,
        ),
        compiler_params=pltpu.CompilerParams(
            collective_id=0, has_side_effects=True, vmem_limit_bytes=48 * 2**20
        ),
    )(
        jnp.transpose(pattern, (0, 3, 1, 2)),
        x_blocks.reshape(blocks, order, width),
        factors.reshape(blocks, levels, 2, order, order),
    )
    return result.reshape(1, 1, blocks, order, width)


def solution(mesh):
    return jax.shard_map(
        on_device,
        mesh=mesh,
        in_specs=(
            P("row", "col", None, None, None),
            P("row", "col", None, None, None, None, None),
            P("row", "col", None, None),
        ),
        out_specs=P("row", "col", None, None, None),
        check_vma=False,
    )
```

time: 160 us -> 152 us (0.950)
  Pallas kernels: 157 us -> 149 us
    pallas_call x1, Pallas kernels: 157 us -> 149 us  [on_device(): pl.pallas_call(kernel, out_shape=jax.ShapeDtypeStruct((blocks, order, wid...]
where the time goes in v3:
time: 152 us; the launch traced here: 151 us
  Pallas kernels  149 us (98%)
  local copies, waits for them, and re-layouts  2.71 us (2%)
    pallas_call x1, Pallas kernels, on_device(): pl.pallas_call(kernel, out_shape=jax.ShapeDtypeStruct((blocks, order, wid...  149 us

profile of v3, /device:TPU:1, one launch (start us, length us, event | category | flops | bytes accessed | tf_op | source)
XLA Modules:
  0.0 151.4 jit_solution(11341847052451314450)
XLA Ops:
  0.0 0.0 copy-start
  0.0 0.7 copy-done
  0.7 148.7 %butterfly.1 = bf16[16,128,1024]{2,1,0:T(8,128)(2,1)S(1)} custom-call(s32[1,11,1,16]{3,2,1,0:T(1,128)S(1)} %bitcast.5, bf16[16,128,1024]{2,1,0:T(8,128)(2,1)} %bitcast.7, bf16[16,11,2,128,128]{4,3,2,1,0:T(8,128)(2,1)} %bitcast.6), custom_call_target="tpu_custom_call" | custom-call | flops 11811160064 | bytes 19922944 | tf_op jit(solution)/shard_map/butterfly/pallas_call | solution.py:415
  149.4 2.0 %copy.5 = bf16[1,1,16,128,1024]{4,3,2,1,0:T(8,128)(2,1)} copy(bf16[1,1,16,128,1024]{4,3,2,1,0:T(8,128)(2,1)S(1)} %bitcast.4) | data formatting | bytes 8388608
Async XLA Ops:
  0.0 0.7 copy-start

commit v4 on v3

--- a/solution.py
+++ b/solution.py
@@ -338,20 +338,28 @@
                     scale(RING, BLOCKS - RING, (4, 5))
                     lax.fori_loop(1, GROUPS, own_z, 0)
 
-                @pl.when(jnp.logical_and(t < 2 * (width // WL - 1), lax.rem(t, 2) == 0))
+                @pl.when(jnp.logical_and(t < 2 * (width // WL - 1), lax.rem(t, 2) == 1))
                 def _():
                     i = lax.div(t, 2) + 1
                     load_x(i).wait()
                     local(i)
 
-                @pl.when(t == 1)
+            if stage is stage_z:
+                @pl.when(t == 2)
                 def _():
-                    for k in range(6, 11):
+                    for k in (6, 7):
                         load_f(k).wait()
-                    scale(0, BLOCKS, (6, 7, 8, 9, 10))
+                    scale(0, BLOCKS, (6, 7))
+                    for g in range(2):
+                        for k in HOPS:
+                            f_x(g, k).start()
+
+                @pl.when(t == 3)
+                def _():
+                    for k in (8, 9, 10):
+                        load_f(k).wait()
+                    scale(0, BLOCKS, (8, 9, 10))
                     for g in range(GROUPS):
-                        for k in HOPS if g < 2 else ():
-                            f_x(g, k).start()
                         for j in range(2):
                             f_c(g, j).start()
                         for k in HOPS:

time: 152 us -> 152 us (level)
  no operation moved by 1% of the time
where the time goes in v4:
time: 152 us; the launch traced here: 151 us
  Pallas kernels  149 us (98%)
  local copies, waits for them, and re-layouts  2.71 us (2%)
    pallas_call x1, Pallas kernels, on_device(): pl.pallas_call(kernel, out_shape=jax.ShapeDtypeStruct((blocks, order, wid...  149 us

profile of v4, /device:TPU:1, one launch (start us, length us, event | category | flops | bytes accessed | tf_op | source)
XLA Modules:
  0.0 151.5 jit_solution(421214691969738655)
XLA Ops:
  0.0 0.0 copy-start
  0.0 0.7 copy-done
  0.7 148.7 %butterfly.1 = bf16[16,128,1024]{2,1,0:T(8,128)(2,1)S(1)} custom-call(s32[1,11,1,16]{3,2,1,0:T(1,128)S(1)} %bitcast.5, bf16[16,128,1024]{2,1,0:T(8,128)(2,1)} %bitcast.7, bf16[16,11,2,128,128]{4,3,2,1,0:T(8,128)(2,1)} %bitcast.6), custom_call_target="tpu_custom_call" | custom-call | flops 11811160064 | bytes 19922944 | tf_op jit(solution)/shard_map/butterfly/pallas_call | solution.py:423
  149.4 2.0 %copy.5 = bf16[1,1,16,128,1024]{4,3,2,1,0:T(8,128)(2,1)} copy(bf16[1,1,16,128,1024]{4,3,2,1,0:T(8,128)(2,1)S(1)} %bitcast.4) | data formatting | bytes 8388608
Async XLA Ops:
  0.0 0.7 copy-start

commit v5 on v4

--- a/solution.py
+++ b/solution.py
@@ -101,10 +101,10 @@
             FAC.at[RING * g + q, 4 + n], FRZ.at[g, z, n], fss.at[0], frs.at[0, g], dev(q, x, y, c)
         )
 
-    def f_x(g, k):
+    def f_x(g, k, n):
         q = far(x, k)
         return send(
-            FAC.at[RING * g + q, 6:8], FRX.at[g, x], fss.at[1], frs.at[1, g], dev(z, q, y, c)
+            FAC.at[RING * g + q, 6 + n], FRX.at[g, x, n], fss.at[1], frs.at[1, g], dev(z, q, y, c)
         )
 
     def f_y(g, k):
@@ -226,9 +226,10 @@
                 def _(k=k, n=n):
                     f_z(g + 1, k, n).start()
 
-            @pl.when(jnp.logical_and(jnp.logical_and(g > 0, g < GROUPS - 1), cc == 2 * i))
-            def _(k=k):
-                f_x(g + 1, k).start()
+                    @pl.when(g > 0)
+                    def _():
+                        f_x(g + 1, k, n).start()
+
 
     def stage_z(u):
         g, cols = place(u)
@@ -352,7 +353,8 @@
                     scale(0, BLOCKS, (6, 7))
                     for g in range(2):
                         for k in HOPS:
-                            f_x(g, k).start()
+                            for n in range(2):
+                                f_x(g, k, n).start()
 
                 @pl.when(t == 3)
                 def _():

time: 152 us -> 152 us (level)
  no operation moved by 1% of the time
where the time goes in v5:
time: 152 us; the launch traced here: 151 us
  Pallas kernels  149 us (98%)
  local copies, waits for them, and re-layouts  2.71 us (2%)
    pallas_call x1, Pallas kernels, on_device(): pl.pallas_call(kernel, out_shape=jax.ShapeDtypeStruct((blocks, order, wid...  149 us

profile of v5, /device:TPU:1, one launch (start us, length us, event | category | flops | bytes accessed | tf_op | source)
XLA Modules:
  0.0 151.5 jit_solution(9014679093335406022)
XLA Ops:
  0.0 0.0 copy-start
  0.0 0.7 copy-done
  0.7 148.7 %butterfly.1 = bf16[16,128,1024]{2,1,0:T(8,128)(2,1)S(1)} custom-call(s32[1,11,1,16]{3,2,1,0:T(1,128)S(1)} %bitcast.5, bf16[16,128,1024]{2,1,0:T(8,128)(2,1)} %bitcast.7, bf16[16,11,2,128,128]{4,3,2,1,0:T(8,128)(2,1)} %bitcast.6), custom_call_target="tpu_custom_call" | custom-call | flops 11811160064 | bytes 19922944 | tf_op jit(solution)/shard_map/butterfly/pallas_call | solution.py:425
  149.4 2.0 %copy.5 = bf16[1,1,16,128,1024]{4,3,2,1,0:T(8,128)(2,1)} copy(bf16[1,1,16,128,1024]{4,3,2,1,0:T(8,128)(2,1)S(1)} %bitcast.4) | data formatting | bytes 8388608
Async XLA Ops:
  0.0 0.7 copy-start
